TPU v7x, 256 devices: a whole 4x4x8 slice. The times are simulated.
256 devices in a mesh: blk: 16 (over z_lo, y, core), ulysses: 16 (over z_hi, x).
Axes of the slice: x: 4, y: 4, z: 8 (z_hi: 4, z_lo: 2; z = z_hi * 2 + z_lo), core: 2. Of those that a mesh axis runs over, the one named last changes fastest.
Arguments:
- query_tokens: bfloat16 [32768, 4096], P(('blk', 'ulysses')), may hold values from -5 to 5
- key_tokens: bfloat16 [32768, 4096], P(('blk', 'ulysses')), may hold values from -5 to 5
- value_tokens: bfloat16 [32768, 4096], P(('blk', 'ulysses')), may hold values from -5 to 5
- cotangent: bfloat16 [32768, 4096], P(('blk', 'ulysses')), may hold values from -5 to 5
- block_mask: int32 [256, 256], replicated, may hold values from 0 to 1, as said below
Outputs:
- attended: bfloat16 [32768, 4096], P(('blk', 'ulysses'))
- grad_query: bfloat16 [32768, 4096], P(('blk', 'ulysses'))
- grad_key: bfloat16 [32768, 4096], P(('blk', 'ulysses'))
- grad_value: bfloat16 [32768, 4096], P(('blk', 'ulysses'))
Inputs may be any that keep to these rules, and one draw needn't show every extreme that they name: block_mask is symmetric. A span is a run of 16 consecutive blocks. Inside a span, block s attends block s2 exactly when they differ by at most one. A query block attends at most one key block in each other span. The queries of one span attend keys of exactly 7 other spans, and at most 2 distinct key blocks of any other span; in every draw some pairs of spans reach 2.
All inputs are finite; a program needn't handle non-finite values.
Results may differ from a plain program's by a relative error of at most 0.0096.
Values may be sent and summed in bfloat16 or wider, within the bound.
A program may use at most 128 MiB of HBM per device.

v0:
```python
import jax
import jax.numpy as jnp
from jax import lax
from jax.sharding import PartitionSpec as P

HEAD_DIM = 128
BLOCK = 128
NEED = 2


def lists_from(flag_rows, list_width):
    columns = flag_rows.shape[-1]
    ranking = flag_rows * columns + (
        columns - 1 - lax.broadcasted_iota(jnp.int32, flag_rows.shape, flag_rows.ndim - 1)
    )
    values_top, indices = lax.top_k(ranking, list_width)
    return (indices, values_top >= columns)


def segment_add(selector, tensor, form):
    return jnp.einsum(form, selector, tensor, precision=lax.Precision.HIGHEST)


def shards(query_tokens, key_tokens, value_tokens, cotangent, block_mask):
    groups = lax.axis_size("blk")
    group_id = lax.axis_index("blk")
    heads_q, heads_k, heads_v, heads_g = (
        lax.all_to_all(query_tokens, "ulysses", split_axis=1, concat_axis=0, tiled=True),
        lax.all_to_all(key_tokens, "ulysses", split_axis=1, concat_axis=0, tiled=True),
        lax.all_to_all(value_tokens, "ulysses", split_axis=1, concat_axis=0, tiled=True),
        lax.all_to_all(cotangent, "ulysses", split_axis=1, concat_axis=0, tiled=True),
    )
    span_len = heads_q.shape[0] // BLOCK
    local_heads = heads_q.shape[1] // HEAD_DIM
    score_scale = HEAD_DIM ** (-0.5)

    def blocked(tensor):
        return tensor.reshape(span_len, BLOCK, local_heads, HEAD_DIM)

    def tokens_of(tensor):
        return tensor.reshape(span_len * BLOCK, local_heads * HEAD_DIM).astype(jnp.bfloat16)

    q_blocks = blocked(heads_q)
    k_blocks = blocked(heads_k)
    v_blocks = blocked(heads_v)
    g_blocks = blocked(heads_g)
    first_row = group_id * span_len
    my_rows = lax.dynamic_slice_in_dim(block_mask, first_row, span_len, 0)
    my_cols = lax.dynamic_slice_in_dim(block_mask, first_row, span_len, 1)
    own_flags = lax.dynamic_slice_in_dim(my_rows, first_row, span_len, 1)
    own_index, own_valid = lists_from(own_flags, 3)
    others = (lax.broadcasted_iota(jnp.int32, (groups, 1), 0) != group_id).astype(jnp.int32)
    row_cube = my_rows.reshape(span_len, groups, span_len)
    fetch_index, fetch_valid = lists_from(jnp.max(row_cube, axis=0) * others, NEED)
    col_cube = my_cols.reshape(groups, span_len, span_len)
    send_index, send_valid = lists_from(jnp.max(col_cube, axis=1) * others, NEED)
    sent_k = k_blocks[send_index]
    sent_v = v_blocks[send_index]
    fetched_k, fetched_v = (
        lax.all_to_all(sent_k, "blk", split_axis=0, concat_axis=0, tiled=True),
        lax.all_to_all(sent_v, "blk", split_axis=0, concat_axis=0, tiled=True),
    )
    spot_iota = lax.broadcasted_iota(jnp.int32, (groups, NEED, span_len), 2)
    fetch_pick = (fetch_index[:, :, None] == spot_iota).astype(jnp.int32)
    attach = jnp.sum(row_cube.transpose(1, 0, 2)[:, None, :, :] * fetch_pick[:, :, None, :], axis=3)
    attach = attach * fetch_valid[:, :, None].astype(jnp.int32)
    query_pick = jnp.sum(attach * spot_iota, axis=2)
    attach_f = attach.astype(jnp.float32)
    own_k = k_blocks[own_index]
    own_v = v_blocks[own_index]
    own_scores = (
        jnp.einsum("irhd,itchd->ithrc", q_blocks, own_k, preferred_element_type=jnp.float32)
        * score_scale
    )
    own_scores = jnp.where(own_valid[:, :, None, None, None], own_scores, -jnp.inf)
    cross_q = q_blocks[query_pick]
    cross_g = g_blocks[query_pick]
    cross_scores = (
        jnp.einsum("curhd,cukhd->cuhrk", cross_q, fetched_k, preferred_element_type=jnp.float32)
        * score_scale
    )
    cross_scores = jnp.where(fetch_valid[:, :, None, None, None], cross_scores, -jnp.inf)
    tile_peak = jnp.max(cross_scores, axis=4)
    cross_peak = jnp.max(
        jnp.where(attach[:, :, :, None, None] > 0, tile_peak[:, :, None], -jnp.inf), axis=(0, 1)
    )
    row_peak = jnp.maximum(jnp.max(own_scores, axis=(1, 4)), cross_peak)
    own_total = jnp.sum(jnp.exp(own_scores - row_peak[:, None, :, :, None]), axis=(1, 4))
    cross_sums = jnp.sum(jnp.exp(cross_scores - row_peak[query_pick][..., None]), axis=4)
    row_total = own_total + segment_add(attach_f, cross_sums, "cui,cuhr->ihr")
    log_total = row_peak + jnp.log(row_total)
    cross_log = log_total[query_pick]
    own_prob = jnp.exp(own_scores - log_total[:, None, :, :, None])
    cross_prob = jnp.exp(cross_scores - cross_log[..., None])
    own_weights = own_prob.astype(jnp.bfloat16)
    cross_weights = cross_prob.astype(jnp.bfloat16)
    cross_out = jnp.einsum(
        "cuhrk,cukhd->curhd", cross_weights, fetched_v, preferred_element_type=jnp.float32
    )
    output = jnp.einsum("ithrc,itchd->irhd", own_weights, own_v, preferred_element_type=jnp.float32)
    output = output + segment_add(attach_f, cross_out, "cui,curhd->irhd")
    row_delta = jnp.sum(g_blocks.astype(jnp.float32) * output, axis=3).transpose(0, 2, 1)
    cross_delta = row_delta[query_pick]
    own_dprob = jnp.einsum("irhd,itchd->ithrc", g_blocks, own_v, preferred_element_type=jnp.float32)
    own_dscore = (own_prob * (own_dprob - row_delta[:, None, :, :, None])).astype(jnp.bfloat16)
    grad_q = score_scale * jnp.einsum(
        "ithrc,itchd->irhd", own_dscore, own_k, preferred_element_type=jnp.float32
    )
    own_dk = score_scale * jnp.einsum(
        "ithrc,irhd->itchd", own_dscore, q_blocks, preferred_element_type=jnp.float32
    )
    own_dv = jnp.einsum(
        "ithrc,irhd->itchd", own_weights, g_blocks, preferred_element_type=jnp.float32
    )
    empty_grad = jnp.zeros((span_len, BLOCK, local_heads, HEAD_DIM), jnp.float32)
    grad_k = empty_grad.at[own_index].add(own_dk)
    grad_v = empty_grad.at[own_index].add(own_dv)
    cross_dprob = jnp.einsum(
        "curhd,cukhd->cuhrk", cross_g, fetched_v, preferred_element_type=jnp.float32
    )
    cross_dscore = (cross_prob * (cross_dprob - cross_delta[..., None])).astype(jnp.bfloat16)
    cross_dq = score_scale * jnp.einsum(
        "cuhrk,cukhd->curhd", cross_dscore, fetched_k, preferred_element_type=jnp.float32
    )
    grad_q = grad_q + segment_add(attach_f, cross_dq, "cui,curhd->irhd")
    part_k = score_scale * jnp.einsum(
        "cuhrk,curhd->cukhd", cross_dscore, cross_q, preferred_element_type=jnp.float32
    )
    part_v = jnp.einsum(
        "cuhrk,curhd->cukhd", cross_weights, cross_g, preferred_element_type=jnp.float32
    )
    back_k, back_v = (
        lax.all_to_all(part_k, "blk", split_axis=0, concat_axis=0, tiled=True),
        lax.all_to_all(part_v, "blk", split_axis=0, concat_axis=0, tiled=True),
    )
    send_pick = ((send_index[:, :, None] == spot_iota) & send_valid[:, :, None]).astype(jnp.float32)
    grad_k = grad_k + segment_add(send_pick, back_k, "buj,bukhd->jkhd")
    grad_v = grad_v + segment_add(send_pick, back_v, "buj,bukhd->jkhd")
    attended, grad_query, grad_key, grad_value = (
        lax.all_to_all(tokens_of(output), "ulysses", split_axis=0, concat_axis=1, tiled=True),
        lax.all_to_all(tokens_of(grad_q), "ulysses", split_axis=0, concat_axis=1, tiled=True),
        lax.all_to_all(tokens_of(grad_k), "ulysses", split_axis=0, concat_axis=1, tiled=True),
        lax.all_to_all(tokens_of(grad_v), "ulysses", split_axis=0, concat_axis=1, tiled=True),
    )
    return (attended, grad_query, grad_key, grad_value)


def solution(mesh):
    placed = (
        P(("blk", "ulysses"), None),
        P(("blk", "ulysses"), None),
        P(("blk", "ulysses"), None),
        P(("blk", "ulysses"), None),
        P(),
    )
    return jax.shard_map(
        shards,
        mesh=mesh,
        in_specs=placed,
        out_specs=(
            P(("blk", "ulysses"), None),
            P(("blk", "ulysses"), None),
            P(("blk", "ulysses"), None),
            P(("blk", "ulysses"), None),
        ),
        check_vma=False,
    )
```

profile of v0, /device:TPU:56, one launch (start us, length us, event | category | flops | bytes accessed | tf_op | source)
XLA Modules:
  0.0 528.4 jit_solution(7634061339372673453)
XLA Ops:
  3.1 10.1 %all-to-all-start.6 = ((bf16[128,16,256]{0,2,1:T(8,128)(2,1)}), bf16[128,16,256]{0,2,1:T(8,128)(2,1)S(1)}, u32[]{:S(2)}, u32[]{:S(2)}) async-start(bf16[128,16,256]{0,2,1:T(8,128)(2,1)} %bitcast.41), calls=%async_computation.6 | async-start | bytes 2097152 | tf_op jit(solution)/shard_map/all_to_all | solution.py:31
  14.5 27.8 %all-to-all-done.6 = bf16[128,16,256]{0,2,1:T(8,128)(2,1)S(1)} async-done(((bf16[128,16,256]{0,2,1:T(8,128)(2,1)}), bf16[128,16,256]{0,2,1:T(8,128)(2,1)S(1)}, u32[]{:S(2)}, u32[]{:S(2)}) %all-to-all-start.6) | async-done | bytes 1048608 | tf_op jit(solution)/shard_map/all_to_all | solution.py:31
  47.8 20.7 %all-to-all-done = bf16[128,16,256]{0,2,1:T(8,128)(2,1)S(1)} async-done(((bf16[128,16,256]{0,2,1:T(8,128)(2,1)}), bf16[128,16,256]{0,2,1:T(8,128)(2,1)S(1)}, u32[]{:S(2)}, u32[]{:S(2)}) %all-to-all-start) | async-done | bytes 1048608 | tf_op jit(solution)/shard_map/all_to_all | solution.py:30
  68.5 10.5 %all-to-all-start.1 = ((bf16[128,16,256]{0,2,1:T(8,128)(2,1)}), bf16[128,16,256]{0,2,1:T(8,128)(2,1)S(1)}, u32[]{:S(2)}, u32[]{:S(2)}) async-start(bf16[128,16,256]{0,2,1:T(8,128)(2,1)} %bitcast.197), calls=%async_computation.1 | async-start | bytes 2097152 | tf_op jit(solution)/shard_map/all_to_all | solution.py:29
  81.3 18.1 %all-to-all-done.1 = bf16[128,16,256]{0,2,1:T(8,128)(2,1)S(1)} async-done(((bf16[128,16,256]{0,2,1:T(8,128)(2,1)}), bf16[128,16,256]{0,2,1:T(8,128)(2,1)S(1)}, u32[]{:S(2)}, u32[]{:S(2)}) %all-to-all-start.1) | async-done | bytes 1048608 | tf_op jit(solution)/shard_map/all_to_all | solution.py:29
  99.3 10.3 %all-to-all-start.2 = ((bf16[128,16,256]{0,2,1:T(8,128)(2,1)}), bf16[128,16,256]{0,2,1:T(8,128)(2,1)S(1)}, u32[]{:S(2)}, u32[]{:S(2)}) async-start(bf16[128,16,256]{0,2,1:T(8,128)(2,1)} %bitcast.195), calls=%async_computation.2 | async-start | bytes 2097152 | tf_op jit(solution)/shard_map/all_to_all | solution.py:28
  115.1 21.1 %all-to-all-done.2 = bf16[128,16,256]{0,2,1:T(8,128)(2,1)S(1)} async-done(((bf16[128,16,256]{0,2,1:T(8,128)(2,1)}), bf16[128,16,256]{0,2,1:T(8,128)(2,1)S(1)}, u32[]{:S(2)}, u32[]{:S(2)}) %all-to-all-start.2) | async-done | bytes 1048608 | tf_op jit(solution)/shard_map/all_to_all | solution.py:28
  151.1 19.7 %all-to-all-done.3 = bf16[16,2,128,2,128]{4,2,3,1,0:T(8,128)(2,1)} async-done(((bf16[16,2,128,2,128]{4,2,3,1,0:T(8,128)(2,1)}), bf16[16,2,128,2,128]{4,2,3,1,0:T(8,128)(2,1)}, u32[]{:S(2)}, u32[]{:S(2)}) %all-to-all-start.3) | async-done | bytes 2097184 | tf_op jit(solution)/shard_map/all_to_all | solution.py:60
  170.8 5.8 %all-to-all-start.4 = ((bf16[16,2,128,2,128]{2,4,3,1,0:T(8,128)(2,1)}), bf16[16,2,128,2,128]{2,4,3,1,0:T(8,128)(2,1)}, u32[]{:S(2)}, u32[]{:S(2)}) async-start(bf16[16,2,128,2,128]{2,4,3,1,0:T(8,128)(2,1)} %bitcast.190), calls=%async_computation.4 | async-start | bytes 4194304 | tf_op jit(solution)/shard_map/all_to_all | solution.py:61
  217.6 6.2 %convolution_bitcast_fusion.2 = f32[16,2,128,2,128]{2,4,3,1,0:T(8,128)} fusion(bf16[16,2,128,2,128]{2,4,3,1,0:T(8,128)(2,1)} %all-to-all-done.4, f32[16,2,2,128,128]{3,4,2,1,0:T(8,128)} %get-tuple-element.58, f32[16,2,2,128]{3,2,1,0:T(2,128)S(1)} %bitcast.198, pred[16,2]{1,0:T(8,128)(4,1)S(1)} %copy.351), kind=kOutput, calls=%fused_computation.36 | convolution fusion | flops 272629760 | bytes 10518560 | tf_op jit(solution)/shard_map/cuhrk,cukhd->curhd/dot_general | solution.py:97
  237.2 7.9 %multiply_reduce_fusion = (f32[16,128,2]{1,2,0:T(2,128)S(1)}, bf16[16,128,2,128]{1,3,2,0:T(8,128)(2,1)}) fusion(bf16[128,16,256]{0,2,1:T(8,128)(2,1)} %copy-done, f32[16,128,2,128]{1,3,2,0:T(8,128)} %copy.374, bf16[16,3,128,2,128]{4,2,1,3,0:T(8,128)(2,1)} %copy.410, f32[16,2,3,128,128]{4,3,2,1,0:T(8,128)} %get-tuple-element.60, ...), kind=kOutput, calls=%fused_computation.41 | convolution fusion | flops 411561984 | bytes 13664304 | tf_op jit(solution)/shard_map/ithrc,itchd->irhd/dot_general | solution.py:100
  259.2 5.8 %fusion.12 = f32[16,128,2,128]{3,0,2,1:T(8,128)} fusion(f32[16,2,128,2,128]{4,2,3,1,0:T(8,128)S(1)} %multiply_bitcast_fusion.2, s32[16,2,16]{2,1,0:T(2,128)S(1)} %multiply_reduce_fusion.1, s32[16,2]{0,1:T(2,128)S(1)} %get-tuple-element.46), kind=kOutput, calls=%fused_computation.42 | convolution fusion | flops 201327616 | bytes 6293632 | tf_op jit(solution)/shard_map/cui,curhd->irhd/dot_general | solution.py:21
  268.0 6.0 %fusion = bf16[16,3,2,128,128]{3,4,1,2,0:T(8,128)(2,1)S(1)} fusion(f32[16,2,3,128,128]{4,3,2,1,0:T(8,128)} %get-tuple-element.60, f32[16,2,128]{2,1,0:T(2,128)S(1)} %bitcast.203, f32[16,2,128]{2,1,0:T(2,128)S(1)} %copy.365, pred[16,3]{1,0:T(8,128)(4,1)S(1)} %copy.340, bf16[16,3,128,2,128]{4,2,1,3,0:T(8,128)(2,1)} %copy.410, ...), kind=kOutput, calls=%fused_computation.12 | convolution fusion | flops 412090368 | bytes 13664304 | tf_op jit(solution)/shard_map/irhd,itchd->ithrc/dot_general | solution.py:104
  281.2 6.5 %all-to-all-start.7 = ((bf16[16,128,256]{1,2,0:T(8,128)(2,1)}), bf16[16,128,256]{1,2,0:T(8,128)(2,1)S(1)}, u32[]{:S(2)}, u32[]{:S(2)}) async-start(bf16[16,128,256]{1,2,0:T(8,128)(2,1)} %bitcast.193), calls=%async_computation.7 | async-start | bytes 2097152 | tf_op jit(solution)/shard_map/all_to_all | solution.py:141
  287.8 5.8 %multiply_bitcast_fusion.1 = f32[16,2,128,2,128]{4,2,3,1,0:T(8,128)} fusion(bf16[16,2,128,2,128]{2,4,3,1,0:T(8,128)(2,1)} %bitcast.184, bf16[16,2,2,128,128]{3,4,2,1,0:T(8,128)(2,1)} %copy-done.6), kind=kOutput, calls=%fused_computation.26 | convolution fusion | flops 269484032 | bytes 8388608 | tf_op jit(solution)/shard_map/cuhrk,curhd->cukhd/dot_general | solution.py:126
  293.5 24.9 %all-to-all-done.7 = bf16[16,128,256]{1,2,0:T(8,128)(2,1)S(1)} async-done(((bf16[16,128,256]{1,2,0:T(8,128)(2,1)}), bf16[16,128,256]{1,2,0:T(8,128)(2,1)S(1)}, u32[]{:S(2)}, u32[]{:S(2)}) %all-to-all-start.7) | async-done | bytes 1048608 | tf_op jit(solution)/shard_map/all_to_all | solution.py:141
  324.2 5.8 %convolution_bitcast_fusion.1 = f32[16,2,128,2,128]{2,4,3,1,0:T(8,128)} fusion(bf16[16,2,128,2,128]{2,4,3,1,0:T(8,128)(2,1)S(1)} %bitcast.187, f32[16,2,2,128,128]{3,4,2,1,0:T(8,128)} %get-tuple-element.58, f32[16,2,2,128]{3,2,1,0:T(2,128)S(1)} %bitcast.200, pred[16,2]{1,0:T(8,128)(4,1)S(1)} %copy.351), kind=kOutput, calls=%fused_computation.35 | convolution fusion | flops 272629760 | bytes 10518560 | tf_op jit(solution)/shard_map/cuhrk,curhd->cukhd/dot_general | solution.py:129
  329.9 55.9 %all-to-all-done.8 = f32[16,2,128,2,128]{4,2,3,1,0:T(8,128)} async-done(((f32[16,2,128,2,128]{4,2,3,1,0:T(8,128)}), f32[16,2,128,2,128]{4,2,3,1,0:T(8,128)}, u32[]{:S(2)}, u32[]{:S(2)}) %all-to-all-start.8) | async-done | bytes 4194336 | tf_op jit(solution)/shard_map/all_to_all | solution.py:133
  397.3 5.9 %fusion.15 = f32[16,128,2,128]{3,0,2,1:T(8,128)S(1)} fusion(f32[16,2,128,2,128]{4,2,3,1,0:T(8,128)} %all-to-all-done.8, s32[16,2]{0,1:T(2,128)S(1)} %get-tuple-element.52, pred[16,2]{0,1:T(4,128)(4,1)S(1)} %slice_compare_fusion.1), kind=kOutput, calls=%fused_computation.43 | convolution fusion | flops 201327616 | bytes 6291616 | tf_op jit(solution)/shard_map/buj,bukhd->jkhd/dot_general | solution.py:21
  404.4 9.4 %scatter_fusion = f32[16,128,2,128]{3,1,2,0:T(8,128)S(1)} fusion(f32[16,128,2,128]{3,1,2,0:T(8,128)S(1)} %copy.396, s32[48]{0:T(128)S(1)} %reshape.124, f32[48,128,2,128]{3,1,2,0:T(8,128)} %bitcast.183), kind=kCustom, calls=%fused_computation.9 | custom fusion | flops 1572864 | bytes 18874560 | tf_op jit(solution)/shard_map/scatter-add | solution.py:116
  417.2 35.7 %all-to-all-done.10 = f32[16,2,128,2,128]{2,4,3,1,0:T(8,128)} async-done(((f32[16,2,128,2,128]{2,4,3,1,0:T(8,128)}), f32[16,2,128,2,128]{2,4,3,1,0:T(8,128)}, u32[]{:S(2)}, u32[]{:S(2)}) %all-to-all-start.10) | async-done | bytes 4194336 | tf_op jit(solution)/shard_map/all_to_all | solution.py:134
  475.6 9.4 %scatter_fusion.1 = f32[16,128,2,128]{3,1,2,0:T(8,128)S(1)} fusion(f32[16,128,2,128]{3,1,2,0:T(8,128)S(1)} %copy.402, s32[48]{0:T(128)S(1)} %reshape.124, f32[48,128,2,128]{3,1,2,0:T(8,128)} %bitcast.182), kind=kCustom, calls=%fused_computation.10 | custom fusion | flops 1572864 | bytes 18874560 | tf_op jit(solution)/shard_map/scatter-add | solution.py:117
  488.9 7.3 %all-to-all-start.11 = ((bf16[16,128,256]{1,2,0:T(8,128)(2,1)}), bf16[16,128,256]{1,2,0:T(8,128)(2,1)S(1)}, u32[]{:S(2)}, u32[]{:S(2)}) async-start(bf16[16,128,256]{1,2,0:T(8,128)(2,1)} %bitcast.78), calls=%async_computation.11 | async-start | bytes 2097152 | tf_op jit(solution)/shard_map/all_to_all | solution.py:143
  502.0 24.8 %all-to-all-done.11 = bf16[16,128,256]{1,2,0:T(8,128)(2,1)S(1)} async-done(((bf16[16,128,256]{1,2,0:T(8,128)(2,1)}), bf16[16,128,256]{1,2,0:T(8,128)(2,1)S(1)}, u32[]{:S(2)}, u32[]{:S(2)}) %all-to-all-start.11) | async-done | bytes 1048608 | tf_op jit(solution)/shard_map/all_to_all | solution.py:143
  (128 shorter events, 165.7 us)
Async XLA Ops:
  0.6 12.6 %copy-start.11 = (bf16[128,4096]{1,0:T(8,128)(2,1)S(1)}, bf16[128,4096]{1,0:T(8,128)(2,1)}, u32[]{:S(2)}) copy-start(bf16[128,4096]{1,0:T(8,128)(2,1)} %param.7) | copy-start | bytes 3145732
  0.6 45.8 %copy-start.12 = (bf16[128,4096]{1,0:T(8,128)(2,1)S(1)}, bf16[128,4096]{1,0:T(8,128)(2,1)}, u32[]{:S(2)}) copy-start(bf16[128,4096]{1,0:T(8,128)(2,1)} %param.6) | copy-start | bytes 3145732
  3.1 39.3 %all-to-all-start.6 = ((bf16[128,16,256]{0,2,1:T(8,128)(2,1)}), bf16[128,16,256]{0,2,1:T(8,128)(2,1)S(1)}, u32[]{:S(2)}, u32[]{:S(2)}) async-start(bf16[128,16,256]{0,2,1:T(8,128)(2,1)} %bitcast.41), calls=%async_computation.6 | async-start | bytes 2097152 | tf_op jit(solution)/shard_map/all_to_all | solution.py:31
  42.3 38.9 %copy-start = (bf16[128,16,256]{0,2,1:T(8,128)(2,1)}, bf16[128,16,256]{0,2,1:T(8,128)(2,1)S(1)}, u32[]{:S(2)}) copy-start(bf16[128,16,256]{0,2,1:T(8,128)(2,1)S(1)} %all-to-all-done.6) | copy-start | bytes 3145732
  42.3 26.2 %all-to-all-start = ((bf16[128,16,256]{0,2,1:T(8,128)(2,1)}), bf16[128,16,256]{0,2,1:T(8,128)(2,1)S(1)}, u32[]{:S(2)}, u32[]{:S(2)}) async-start(bf16[128,16,256]{0,2,1:T(8,128)(2,1)} %bitcast), calls=%async_computation | async-start | bytes 2097152 | tf_op jit(solution)/shard_map/all_to_all | solution.py:30
  46.4 63.2 %copy-start.13 = (s32[256,256]{1,0:T(8,128)S(1)}, s32[256,256]{1,0:T(8,128)}, u32[]{:S(2)}) copy-start(s32[256,256]{1,0:T(8,128)} %param.9) | copy-start | bytes 786436
  68.5 30.9 %all-to-all-start.1 = ((bf16[128,16,256]{0,2,1:T(8,128)(2,1)}), bf16[128,16,256]{0,2,1:T(8,128)(2,1)S(1)}, u32[]{:S(2)}, u32[]{:S(2)}) async-start(bf16[128,16,256]{0,2,1:T(8,128)(2,1)} %bitcast.197), calls=%async_computation.1 | async-start | bytes 2097152 | tf_op jit(solution)/shard_map/all_to_all | solution.py:29
  99.3 36.9 %all-to-all-start.2 = ((bf16[128,16,256]{0,2,1:T(8,128)(2,1)}), bf16[128,16,256]{0,2,1:T(8,128)(2,1)S(1)}, u32[]{:S(2)}, u32[]{:S(2)}) async-start(bf16[128,16,256]{0,2,1:T(8,128)(2,1)} %bitcast.195), calls=%async_computation.2 | async-start | bytes 2097152 | tf_op jit(solution)/shard_map/all_to_all | solution.py:28
  136.2 10.8 %copy-start.2 = (bf16[128,16,256]{0,2,1:T(8,128)(2,1)}, bf16[128,16,256]{0,2,1:T(8,128)(2,1)S(1)}, u32[]{:S(2)}) copy-start(bf16[128,16,256]{0,2,1:T(8,128)(2,1)S(1)} %all-to-all-done.2) | copy-start | bytes 3145732
  136.2 34.6 %all-to-all-start.3 = ((bf16[16,2,128,2,128]{4,2,3,1,0:T(8,128)(2,1)}), bf16[16,2,128,2,128]{4,2,3,1,0:T(8,128)(2,1)}, u32[]{:S(2)}, u32[]{:S(2)}) async-start(bf16[16,2,128,2,128]{4,2,3,1,0:T(8,128)(2,1)} %bitcast.191), calls=%async_computation.3 | async-start | bytes 4194304 | tf_op jit(solution)/shard_map/all_to_all | solution.py:60
  170.8 46.8 %all-to-all-start.4 = ((bf16[16,2,128,2,128]{2,4,3,1,0:T(8,128)(2,1)}), bf16[16,2,128,2,128]{2,4,3,1,0:T(8,128)(2,1)}, u32[]{:S(2)}, u32[]{:S(2)}) async-start(bf16[16,2,128,2,128]{2,4,3,1,0:T(8,128)(2,1)} %bitcast.190), calls=%async_computation.4 | async-start | bytes 4194304 | tf_op jit(solution)/shard_map/all_to_all | solution.py:61
  198.6 5.0 copy-start.4
  245.2 36.1 %all-to-all-start.5 = ((bf16[16,128,256]{1,2,0:T(8,128)(2,1)}), bf16[16,128,256]{1,2,0:T(8,128)(2,1)}, u32[]{:S(2)}, u32[]{:S(2)}) async-start(bf16[16,128,256]{1,2,0:T(8,128)(2,1)} %bitcast.192), calls=%async_computation.5 | async-start | bytes 2097152 | tf_op jit(solution)/shard_map/all_to_all | solution.py:140
  268.0 7.6 %copy-start.8 = (f32[16,128,2,128]{1,3,2,0:T(8,128)S(1)}, f32[16,128,2,128]{1,3,2,0:T(8,128)}, u32[]{:S(2)}) copy-start(f32[16,128,2,128]{1,3,2,0:T(8,128)} %copy.389) | copy-start | bytes 6291460
  281.2 37.2 %all-to-all-start.7 = ((bf16[16,128,256]{1,2,0:T(8,128)(2,1)}), bf16[16,128,256]{1,2,0:T(8,128)(2,1)S(1)}, u32[]{:S(2)}, u32[]{:S(2)}) async-start(bf16[16,128,256]{1,2,0:T(8,128)(2,1)} %bitcast.193), calls=%async_computation.7 | async-start | bytes 2097152 | tf_op jit(solution)/shard_map/all_to_all | solution.py:141
  293.5 30.6 %copy-start.5 = (bf16[32,128,2,128]{1,3,2,0:T(8,128)(2,1)S(1)}, bf16[32,128,2,128]{1,3,2,0:T(8,128)(2,1)}, u32[]{:S(2)}) copy-start(bf16[32,128,2,128]{1,3,2,0:T(8,128)(2,1)} %gather_fusion.7) | copy-start | bytes 6291460
  318.4 11.5 %copy-start.9 = (bf16[16,128,256]{1,2,0:T(8,128)(2,1)}, bf16[16,128,256]{1,2,0:T(8,128)(2,1)S(1)}, u32[]{:S(2)}) copy-start(bf16[16,128,256]{1,2,0:T(8,128)(2,1)S(1)} %all-to-all-done.7) | copy-start | bytes 3145732
  318.4 67.4 %all-to-all-start.8 = ((f32[16,2,128,2,128]{4,2,3,1,0:T(8,128)}), f32[16,2,128,2,128]{4,2,3,1,0:T(8,128)}, u32[]{:S(2)}, u32[]{:S(2)}) async-start(f32[16,2,128,2,128]{4,2,3,1,0:T(8,128)} %multiply_bitcast_fusion.1), calls=%async_computation.8 | async-start | bytes 8388608 | tf_op jit(solution)/shard_map/all_to_all | solution.py:133
  329.9 61.3 %copy-start.3 = (bf16[128,16,256]{0,2,1:T(8,128)(2,1)S(1)}, bf16[128,16,256]{0,2,1:T(8,128)(2,1)}, u32[]{:S(2)}) copy-start(bf16[128,16,256]{0,2,1:T(8,128)(2,1)} %copy-done.2) | copy-start | bytes 3145732
  385.8 67.1 %all-to-all-start.10 = ((f32[16,2,128,2,128]{2,4,3,1,0:T(8,128)}), f32[16,2,128,2,128]{2,4,3,1,0:T(8,128)}, u32[]{:S(2)}, u32[]{:S(2)}) async-start(f32[16,2,128,2,128]{2,4,3,1,0:T(8,128)} %convolution_bitcast_fusion.1), calls=%async_computation.10 | async-start | bytes 8388608 | tf_op jit(solution)/shard_map/all_to_all | solution.py:134
  413.8 43.7 %copy-start.1 = (bf16[128,16,256]{0,2,1:T(8,128)(2,1)S(1)}, bf16[128,16,256]{0,2,1:T(8,128)(2,1)}, u32[]{:S(2)}) copy-start(bf16[128,16,256]{0,2,1:T(8,128)(2,1)} %copy-done) | copy-start | bytes 3145732
  452.9 36.0 %all-to-all-start.9 = ((bf16[16,128,256]{1,2,0:T(8,128)(2,1)}), bf16[16,128,256]{1,2,0:T(8,128)(2,1)}, u32[]{:S(2)}, u32[]{:S(2)}) async-start(bf16[16,128,256]{1,2,0:T(8,128)(2,1)} %bitcast.68), calls=%async_computation.9 | async-start | bytes 2097152 | tf_op jit(solution)/shard_map/all_to_all | solution.py:142
  485.2 13.3 %copy-start.10 = (bf16[16,128,256]{1,2,0:T(8,128)(2,1)S(1)}, bf16[16,128,256]{1,2,0:T(8,128)(2,1)}, u32[]{:S(2)}) copy-start(bf16[16,128,256]{1,2,0:T(8,128)(2,1)} %copy-done.9) | copy-start | bytes 3145732
  488.9 37.9 %all-to-all-start.11 = ((bf16[16,128,256]{1,2,0:T(8,128)(2,1)}), bf16[16,128,256]{1,2,0:T(8,128)(2,1)S(1)}, u32[]{:S(2)}, u32[]{:S(2)}) async-start(bf16[16,128,256]{1,2,0:T(8,128)(2,1)} %bitcast.78), calls=%async_computation.11 | async-start | bytes 2097152 | tf_op jit(solution)/shard_map/all_to_all | solution.py:143
  (2 other events, 4.9 us)
where the time goes:
time: 534 us; the launch traced here: 528 us
  waiting for transfers between devices  254 us (48%)
  local copies, waits for them, and re-layouts  82.5 us (15%)
  starting transfers between devices  80.7 us (15%)
  matrix products  79.8 us (15%)
  other arithmetic  29.6 us (6%)
    all_to_all x1, waiting for transfers between devices, shards(): lax.all_to_all(part_k, 'blk', split_axis=0, concat_axis=0, tiled=True)  55.9 us
    all_to_all x1, waiting for transfers between devices, shards(): lax.all_to_all(part_v, 'blk', split_axis=0, concat_axis=0, tiled=True)  35.7 us
    all_to_all x1, waiting for transfers between devices, shards(): lax.all_to_all(cotangent, 'ulysses', split_axis=1, concat_axis=0, tiled=T...  27.8 us
    all_to_all x1, waiting for transfers between devices, shards(): lax.all_to_all(tokens_of(grad_q), 'ulysses', split_axis=0, concat_axis=1,...  24.9 us
    all_to_all x1, waiting for transfers between devices, shards(): lax.all_to_all(tokens_of(grad_v), 'ulysses', split_axis=0, concat_axis=1,...  24.8 us
    all_to_all x1, waiting for transfers between devices, shards(): lax.all_to_all(query_tokens, 'ulysses', split_axis=1, concat_axis=0, tile...  21.1 us
    dot_general x5, matrix products, segment_add(): return jnp.einsum(form, selector, tensor, precision=lax.Precision.HIGHEST)  20.8 us
    all_to_all x1, waiting for transfers between devices, shards(): lax.all_to_all(value_tokens, 'ulysses', split_axis=1, concat_axis=0, tile...  20.7 us
  transfers between devices with their start and end apart: 12, of which 11 were waited for; matrix products, arithmetic and copies ran while one was open for 30% of the time, Pallas kernels for 0%

commit v1 on v0

--- a/solution.py
+++ b/solution.py
@@ -28,7 +28,12 @@
         lax.all_to_all(query_tokens, "ulysses", split_axis=1, concat_axis=0, tiled=True),
         lax.all_to_all(key_tokens, "ulysses", split_axis=1, concat_axis=0, tiled=True),
         lax.all_to_all(value_tokens, "ulysses", split_axis=1, concat_axis=0, tiled=True),
-        lax.all_to_all(cotangent, "ulysses", split_axis=1, concat_axis=0, tiled=True),
+        jnp.concatenate(
+            lax.all_to_all(
+                jnp.stack(jnp.split(cotangent, lax.psum(1, "ulysses"), axis=1)), "ulysses", 0, 0
+            ),
+            axis=0,
+        ),
     )
     span_len = heads_q.shape[0] // BLOCK
     local_heads = heads_q.shape[1] // HEAD_DIM

time: 534 us -> 565 us (1.058)
  local copies, waits for them, and re-layouts: 82.5 us -> 109 us
    unnamed x33 -> x48, local copies, waits for them, and re-layouts: 10.1 us -> 32.3 us
  transfers between devices with their start and end apart: 12 -> 12, of which waited for: 11 -> 10; matrix products, arithmetic and copies ran while one was open for 30% -> 30% of each run, Pallas kernels for 0% -> 0%
where the time goes in v1:
time: 565 us; the launch traced here: 558 us
  waiting for transfers between devices  252 us (45%)
  local copies, waits for them, and re-layouts  109 us (19%)
  starting transfers between devices  83 us (15%)
  matrix products  82.6 us (15%)
  other arithmetic  29.6 us (5%)
    all_to_all x1, waiting for transfers between devices, shards(): lax.all_to_all(part_k, 'blk', split_axis=0, concat_axis=0, tiled=True)  55.9 us
    all_to_all x1, waiting for transfers between devices, shards(): lax.all_to_all(part_v, 'blk', split_axis=0, concat_axis=0, tiled=True)  35.7 us
    unnamed x48, local copies, waits for them, and re-layouts  32.3 us
    all_to_all x1, waiting for transfers between devices, shards(): lax.all_to_all(jnp.stack(jnp.split(cotangent, lax.psum(1, 'ulysses'), axi...  27.8 us
    all_to_all x1, waiting for transfers between devices, shards(): lax.all_to_all(tokens_of(grad_q), 'ulysses', split_axis=0, concat_axis=1,...  24.9 us
    all_to_all x1, waiting for transfers between devices, shards(): lax.all_to_all(tokens_of(grad_v), 'ulysses', split_axis=0, concat_axis=1,...  24.8 us
    dot_general x5, matrix products, segment_add(): return jnp.einsum(form, selector, tensor, precision=lax.Precision.HIGHEST)  20.8 us
    all_to_all x1, waiting for transfers between devices, shards(): lax.all_to_all(query_tokens, 'ulysses', split_axis=1, concat_axis=0, tile...  20.7 us
  transfers between devices with their start and end apart: 12, of which 10 were waited for; matrix products, arithmetic and copies ran while one was open for 30% of the time, Pallas kernels for 0%

profile of v1, /device:TPU:56, one launch (start us, length us, event | category | flops | bytes accessed | tf_op | source)
XLA Modules:
  0.0 558.0 jit_solution(9600516541435589476)
XLA Ops:
  24.4 10.1 %all-to-all-start.6 = ((bf16[16,128,256]{2,1,0:T(8,128)(2,1)}), bf16[16,128,256]{2,1,0:T(8,128)(2,1)S(1)}, u32[]{:S(2)}, u32[]{:S(2)}) async-start(bf16[16,128,256]{2,1,0:T(8,128)(2,1)} %bitcast_dynamic-update-slice_fusion), calls=%async_computation.6 | async-start | bytes 2097152 | tf_op jit(solution)/shard_map/all_to_all | solution.py:32
  35.8 27.8 %all-to-all-done.6 = bf16[16,128,256]{2,1,0:T(8,128)(2,1)S(1)} async-done(((bf16[16,128,256]{2,1,0:T(8,128)(2,1)}), bf16[16,128,256]{2,1,0:T(8,128)(2,1)S(1)}, u32[]{:S(2)}, u32[]{:S(2)}) %all-to-all-start.6) | async-done | bytes 1048608 | tf_op jit(solution)/shard_map/all_to_all | solution.py:32
  69.1 20.7 %all-to-all-done = bf16[128,16,256]{0,2,1:T(8,128)(2,1)S(1)} async-done(((bf16[128,16,256]{0,2,1:T(8,128)(2,1)}), bf16[128,16,256]{0,2,1:T(8,128)(2,1)S(1)}, u32[]{:S(2)}, u32[]{:S(2)}) %all-to-all-start) | async-done | bytes 1048608 | tf_op jit(solution)/shard_map/all_to_all | solution.py:30
  89.8 10.5 %all-to-all-start.1 = ((bf16[128,16,256]{0,2,1:T(8,128)(2,1)}), bf16[128,16,256]{0,2,1:T(8,128)(2,1)S(1)}, u32[]{:S(2)}, u32[]{:S(2)}) async-start(bf16[128,16,256]{0,2,1:T(8,128)(2,1)} %bitcast.228), calls=%async_computation.1 | async-start | bytes 2097152 | tf_op jit(solution)/shard_map/all_to_all | solution.py:29
  102.6 18.1 %all-to-all-done.1 = bf16[128,16,256]{0,2,1:T(8,128)(2,1)S(1)} async-done(((bf16[128,16,256]{0,2,1:T(8,128)(2,1)}), bf16[128,16,256]{0,2,1:T(8,128)(2,1)S(1)}, u32[]{:S(2)}, u32[]{:S(2)}) %all-to-all-start.1) | async-done | bytes 1048608 | tf_op jit(solution)/shard_map/all_to_all | solution.py:29
  120.6 10.3 %all-to-all-start.2 = ((bf16[128,16,256]{0,2,1:T(8,128)(2,1)}), bf16[128,16,256]{0,2,1:T(8,128)(2,1)S(1)}, u32[]{:S(2)}, u32[]{:S(2)}) async-start(bf16[128,16,256]{0,2,1:T(8,128)(2,1)} %bitcast.226), calls=%async_computation.2 | async-start | bytes 2097152 | tf_op jit(solution)/shard_map/all_to_all | solution.py:28
  136.8 20.7 %all-to-all-done.2 = bf16[128,16,256]{0,2,1:T(8,128)(2,1)S(1)} async-done(((bf16[128,16,256]{0,2,1:T(8,128)(2,1)}), bf16[128,16,256]{0,2,1:T(8,128)(2,1)S(1)}, u32[]{:S(2)}, u32[]{:S(2)}) %all-to-all-start.2) | async-done | bytes 1048608 | tf_op jit(solution)/shard_map/all_to_all | solution.py:28
  171.9 20.2 %all-to-all-done.3 = bf16[16,2,128,2,128]{4,2,3,1,0:T(8,128)(2,1)} async-done(((bf16[16,2,128,2,128]{4,2,3,1,0:T(8,128)(2,1)}), bf16[16,2,128,2,128]{4,2,3,1,0:T(8,128)(2,1)}, u32[]{:S(2)}, u32[]{:S(2)}) %all-to-all-start.3) | async-done | bytes 2097184 | tf_op jit(solution)/shard_map/all_to_all | solution.py:65
  241.4 6.2 %convolution_bitcast_fusion.2 = f32[16,2,128,2,128]{2,4,3,1,0:T(8,128)} fusion(bf16[16,2,128,2,128]{2,4,3,1,0:T(8,128)(2,1)} %all-to-all-done.4, f32[16,2,2,128,128]{3,4,2,1,0:T(8,128)} %get-tuple-element.58, f32[16,2,2,128]{3,2,1,0:T(2,128)S(1)} %bitcast.229, pred[16,2]{1,0:T(8,128)(4,1)S(1)} %copy.351), kind=kOutput, calls=%fused_computation.36 | convolution fusion | flops 272629760 | bytes 10518560 | tf_op jit(solution)/shard_map/cuhrk,cukhd->curhd/dot_general | solution.py:102
  261.0 7.9 %multiply_reduce_fusion = (f32[16,128,2]{1,2,0:T(2,128)S(1)}, bf16[16,128,2,128]{1,3,2,0:T(8,128)(2,1)}) fusion(bf16[16,128,256]{1,2,0:T(8,128)(2,1)} %copy.376, f32[16,128,2,128]{1,3,2,0:T(8,128)} %copy.374, bf16[16,3,128,2,128]{4,2,1,3,0:T(8,128)(2,1)} %copy.410, f32[16,2,3,128,128]{4,3,2,1,0:T(8,128)} %get-tuple-element.60, ...), kind=kOutput, calls=%fused_computation.41 | convolution fusion | flops 411561984 | bytes 13664304 | tf_op jit(solution)/shard_map/ithrc,itchd->irhd/dot_general | solution.py:105
  282.9 5.8 %fusion.12 = f32[16,128,2,128]{3,0,2,1:T(8,128)} fusion(f32[16,2,128,2,128]{4,2,3,1,0:T(8,128)S(1)} %multiply_bitcast_fusion.2, s32[16,2,16]{2,1,0:T(2,128)S(1)} %multiply_reduce_fusion.1, s32[16,2]{0,1:T(2,128)S(1)} %get-tuple-element.46), kind=kOutput, calls=%fused_computation.42 | convolution fusion | flops 201327616 | bytes 6293632 | tf_op jit(solution)/shard_map/cui,curhd->irhd/dot_general | solution.py:21
  291.7 6.0 %fusion = bf16[16,3,2,128,128]{3,4,1,2,0:T(8,128)(2,1)S(1)} fusion(f32[16,2,3,128,128]{4,3,2,1,0:T(8,128)} %get-tuple-element.60, f32[16,2,128]{2,1,0:T(2,128)S(1)} %bitcast.234, f32[16,2,128]{2,1,0:T(2,128)S(1)} %copy.365, pred[16,3]{1,0:T(8,128)(4,1)S(1)} %copy.340, bf16[16,3,128,2,128]{4,2,1,3,0:T(8,128)(2,1)} %copy.410, ...), kind=kOutput, calls=%fused_computation.12 | convolution fusion | flops 412090368 | bytes 13664304 | tf_op jit(solution)/shard_map/irhd,itchd->ithrc/dot_general | solution.py:109
  304.9 6.5 %all-to-all-start.7 = ((bf16[16,128,256]{1,2,0:T(8,128)(2,1)}), bf16[16,128,256]{1,2,0:T(8,128)(2,1)S(1)}, u32[]{:S(2)}, u32[]{:S(2)}) async-start(bf16[16,128,256]{1,2,0:T(8,128)(2,1)} %bitcast.224), calls=%async_computation.7 | async-start | bytes 2097152 | tf_op jit(solution)/shard_map/all_to_all | solution.py:146
  317.2 24.9 %all-to-all-done.7 = bf16[16,128,256]{1,2,0:T(8,128)(2,1)S(1)} async-done(((bf16[16,128,256]{1,2,0:T(8,128)(2,1)}), bf16[16,128,256]{1,2,0:T(8,128)(2,1)S(1)}, u32[]{:S(2)}, u32[]{:S(2)}) %all-to-all-start.7) | async-done | bytes 1048608 | tf_op jit(solution)/shard_map/all_to_all | solution.py:146
  347.9 5.8 %convolution_bitcast_fusion.1 = f32[16,2,128,2,128]{2,4,3,1,0:T(8,128)} fusion(bf16[16,2,128,2,128]{2,4,3,1,0:T(8,128)(2,1)S(1)} %bitcast.218, f32[16,2,2,128,128]{3,4,2,1,0:T(8,128)} %get-tuple-element.58, f32[16,2,2,128]{3,2,1,0:T(2,128)S(1)} %bitcast.231, pred[16,2]{1,0:T(8,128)(4,1)S(1)} %copy.351), kind=kOutput, calls=%fused_computation.35 | convolution fusion | flops 272629760 | bytes 10518560 | tf_op jit(solution)/shard_map/cuhrk,curhd->cukhd/dot_general | solution.py:134
  353.6 55.9 %all-to-all-done.8 = f32[16,2,128,2,128]{4,2,3,1,0:T(8,128)} async-done(((f32[16,2,128,2,128]{4,2,3,1,0:T(8,128)}), f32[16,2,128,2,128]{4,2,3,1,0:T(8,128)}, u32[]{:S(2)}, u32[]{:S(2)}) %all-to-all-start.8) | async-done | bytes 4194336 | tf_op jit(solution)/shard_map/all_to_all | solution.py:138
  421.0 5.9 %fusion.15 = f32[16,128,2,128]{3,0,2,1:T(8,128)S(1)} fusion(f32[16,2,128,2,128]{4,2,3,1,0:T(8,128)} %all-to-all-done.8, s32[16,2]{0,1:T(2,128)S(1)} %get-tuple-element.52, pred[16,2]{0,1:T(4,128)(4,1)S(1)} %slice_compare_fusion.1), kind=kOutput, calls=%fused_computation.43 | convolution fusion | flops 201327616 | bytes 6291616 | tf_op jit(solution)/shard_map/buj,bukhd->jkhd/dot_general | solution.py:21
  428.1 9.4 %scatter_fusion = f32[16,128,2,128]{3,1,2,0:T(8,128)S(1)} fusion(f32[16,128,2,128]{3,1,2,0:T(8,128)S(1)} %copy.396, s32[48]{0:T(128)S(1)} %reshape.116, f32[48,128,2,128]{3,1,2,0:T(8,128)} %bitcast.214), kind=kCustom, calls=%fused_computation.9 | custom fusion | flops 1572864 | bytes 18874560 | tf_op jit(solution)/shard_map/scatter-add | solution.py:121
  440.9 35.7 %all-to-all-done.10 = f32[16,2,128,2,128]{2,4,3,1,0:T(8,128)} async-done(((f32[16,2,128,2,128]{2,4,3,1,0:T(8,128)}), f32[16,2,128,2,128]{2,4,3,1,0:T(8,128)}, u32[]{:S(2)}, u32[]{:S(2)}) %all-to-all-start.10) | async-done | bytes 4194336 | tf_op jit(solution)/shard_map/all_to_all | solution.py:139
  481.2 6.9 %convolution_bitcast_fusion = f32[16,3,128,2,128]{2,4,1,3,0:T(8,128)} fusion(bf16[16,128,2,128,1]{1,3,4,2,0:T(8,128)(2,1)S(1)} %bitcast.213, f32[16,2,3,128,128]{4,3,2,1,0:T(8,128)} %get-tuple-element.60, f32[16,2,128]{2,1,0:T(2,128)S(1)} %copy.365, pred[16,3]{1,0:T(8,128)(4,1)S(1)} %copy.340), kind=kOutput, calls=%fused_computation.34 | convolution fusion | flops 408944640 | bytes 13647920 | tf_op jit(solution)/shard_map/ithrc,irhd->itchd/dot_general | solution.py:117
  488.1 6.6 %copy.401 = f32[16,3,128,2,128]{4,2,3,1,0:T(8,128)} copy(f32[16,3,128,2,128]{2,4,1,3,0:T(8,128)} %convolution_bitcast_fusion) | data formatting | bytes 12582912 | tf_op jit(solution)/shard_map/ithrc,irhd->itchd/transpose | solution.py:117
  505.3 9.4 %scatter_fusion.1 = f32[16,128,2,128]{3,1,2,0:T(8,128)S(1)} fusion(f32[16,128,2,128]{3,1,2,0:T(8,128)S(1)} %copy.402, s32[48]{0:T(128)S(1)} %reshape.116, f32[48,128,2,128]{3,1,2,0:T(8,128)} %bitcast.203), kind=kCustom, calls=%fused_computation.10 | custom fusion | flops 1572864 | bytes 18874560 | tf_op jit(solution)/shard_map/scatter-add | solution.py:122
  516.2 9.7 %all-to-all-start.11 = ((bf16[16,128,256]{1,2,0:T(8,128)(2,1)}), bf16[16,128,256]{1,2,0:T(8,128)(2,1)S(1)}, u32[]{:S(2)}, u32[]{:S(2)}) async-start(bf16[16,128,256]{1,2,0:T(8,128)(2,1)} %bitcast.92), calls=%async_computation.11 | async-start | bytes 2097152 | tf_op jit(solution)/shard_map/all_to_all | solution.py:148
  531.7 24.8 %all-to-all-done.11 = bf16[16,128,256]{1,2,0:T(8,128)(2,1)S(1)} async-done(((bf16[16,128,256]{1,2,0:T(8,128)(2,1)}), bf16[16,128,256]{1,2,0:T(8,128)(2,1)S(1)}, u32[]{:S(2)}, u32[]{:S(2)}) %all-to-all-start.11) | async-done | bytes 1048608 | tf_op jit(solution)/shard_map/all_to_all | solution.py:148
  (143 shorter events, 190.8 us)
Async XLA Ops:
  0.6 33.9 %copy-start.11 = (bf16[128,4096]{1,0:T(8,128)(2,1)S(1)}, bf16[128,4096]{1,0:T(8,128)(2,1)}, u32[]{:S(2)}) copy-start(bf16[128,4096]{1,0:T(8,128)(2,1)} %param.7) | copy-start | bytes 3145732
  0.6 67.1 %copy-start.12 = (bf16[128,4096]{1,0:T(8,128)(2,1)S(1)}, bf16[128,4096]{1,0:T(8,128)(2,1)}, u32[]{:S(2)}) copy-start(bf16[128,4096]{1,0:T(8,128)(2,1)} %param.6) | copy-start | bytes 3145732
  24.4 39.3 %all-to-all-start.6 = ((bf16[16,128,256]{2,1,0:T(8,128)(2,1)}), bf16[16,128,256]{2,1,0:T(8,128)(2,1)S(1)}, u32[]{:S(2)}, u32[]{:S(2)}) async-start(bf16[16,128,256]{2,1,0:T(8,128)(2,1)} %bitcast_dynamic-update-slice_fusion), calls=%async_computation.6 | async-start | bytes 2097152 | tf_op jit(solution)/shard_map/all_to_all | solution.py:32
  63.6 38.9 %copy-start.8 = (bf16[16,128,256]{2,1,0:T(8,128)(2,1)}, bf16[16,128,256]{2,1,0:T(8,128)(2,1)S(1)}, u32[]{:S(2)}) copy-start(bf16[16,128,256]{2,1,0:T(8,128)(2,1)S(1)} %all-to-all-done.6) | copy-start | bytes 3145732
  63.6 26.2 %all-to-all-start = ((bf16[128,16,256]{0,2,1:T(8,128)(2,1)}), bf16[128,16,256]{0,2,1:T(8,128)(2,1)S(1)}, u32[]{:S(2)}, u32[]{:S(2)}) async-start(bf16[128,16,256]{0,2,1:T(8,128)(2,1)} %bitcast), calls=%async_computation | async-start | bytes 2097152 | tf_op jit(solution)/shard_map/all_to_all | solution.py:30
  67.8 63.2 %copy-start.13 = (s32[256,256]{1,0:T(8,128)S(1)}, s32[256,256]{1,0:T(8,128)}, u32[]{:S(2)}) copy-start(s32[256,256]{1,0:T(8,128)} %param.9) | copy-start | bytes 786436
  89.8 30.9 %all-to-all-start.1 = ((bf16[128,16,256]{0,2,1:T(8,128)(2,1)}), bf16[128,16,256]{0,2,1:T(8,128)(2,1)S(1)}, u32[]{:S(2)}, u32[]{:S(2)}) async-start(bf16[128,16,256]{0,2,1:T(8,128)(2,1)} %bitcast.228), calls=%async_computation.1 | async-start | bytes 2097152 | tf_op jit(solution)/shard_map/all_to_all | solution.py:29
  120.6 36.9 %all-to-all-start.2 = ((bf16[128,16,256]{0,2,1:T(8,128)(2,1)}), bf16[128,16,256]{0,2,1:T(8,128)(2,1)S(1)}, u32[]{:S(2)}, u32[]{:S(2)}) async-start(bf16[128,16,256]{0,2,1:T(8,128)(2,1)} %bitcast.226), calls=%async_computation.2 | async-start | bytes 2097152 | tf_op jit(solution)/shard_map/all_to_all | solution.py:28
  157.5 10.3 %copy-start = (bf16[128,16,256]{0,2,1:T(8,128)(2,1)}, bf16[128,16,256]{0,2,1:T(8,128)(2,1)S(1)}, u32[]{:S(2)}) copy-start(bf16[128,16,256]{0,2,1:T(8,128)(2,1)S(1)} %all-to-all-done.2) | copy-start | bytes 3145732
  157.5 34.6 %all-to-all-start.3 = ((bf16[16,2,128,2,128]{4,2,3,1,0:T(8,128)(2,1)}), bf16[16,2,128,2,128]{4,2,3,1,0:T(8,128)(2,1)}, u32[]{:S(2)}, u32[]{:S(2)}) async-start(bf16[16,2,128,2,128]{4,2,3,1,0:T(8,128)(2,1)} %bitcast.222), calls=%async_computation.3 | async-start | bytes 4194304 | tf_op jit(solution)/shard_map/all_to_all | solution.py:65
  192.1 49.3 %all-to-all-start.4 = ((bf16[16,2,128,2,128]{2,4,3,1,0:T(8,128)(2,1)}), bf16[16,2,128,2,128]{2,4,3,1,0:T(8,128)(2,1)}, u32[]{:S(2)}, u32[]{:S(2)}) async-start(bf16[16,2,128,2,128]{2,4,3,1,0:T(8,128)(2,1)} %bitcast.221), calls=%async_computation.4 | async-start | bytes 4194304 | tf_op jit(solution)/shard_map/all_to_all | solution.py:66
  222.3 5.0 copy-start.3
  268.9 36.1 %all-to-all-start.5 = ((bf16[16,128,256]{1,2,0:T(8,128)(2,1)}), bf16[16,128,256]{1,2,0:T(8,128)(2,1)}, u32[]{:S(2)}, u32[]{:S(2)}) async-start(bf16[16,128,256]{1,2,0:T(8,128)(2,1)} %bitcast.223), calls=%async_computation.5 | async-start | bytes 2097152 | tf_op jit(solution)/shard_map/all_to_all | solution.py:145
  291.7 7.6 %copy-start.7 = (f32[16,128,2,128]{1,3,2,0:T(8,128)S(1)}, f32[16,128,2,128]{1,3,2,0:T(8,128)}, u32[]{:S(2)}) copy-start(f32[16,128,2,128]{1,3,2,0:T(8,128)} %copy.389) | copy-start | bytes 6291460
  304.9 37.2 %all-to-all-start.7 = ((bf16[16,128,256]{1,2,0:T(8,128)(2,1)}), bf16[16,128,256]{1,2,0:T(8,128)(2,1)S(1)}, u32[]{:S(2)}, u32[]{:S(2)}) async-start(bf16[16,128,256]{1,2,0:T(8,128)(2,1)} %bitcast.224), calls=%async_computation.7 | async-start | bytes 2097152 | tf_op jit(solution)/shard_map/all_to_all | solution.py:146
  317.2 30.6 %copy-start.4 = (bf16[32,128,2,128]{1,3,2,0:T(8,128)(2,1)S(1)}, bf16[32,128,2,128]{1,3,2,0:T(8,128)(2,1)}, u32[]{:S(2)}) copy-start(bf16[32,128,2,128]{1,3,2,0:T(8,128)(2,1)} %gather_fusion.7) | copy-start | bytes 6291460
  342.1 11.5 %copy-start.9 = (bf16[16,128,256]{1,2,0:T(8,128)(2,1)}, bf16[16,128,256]{1,2,0:T(8,128)(2,1)S(1)}, u32[]{:S(2)}) copy-start(bf16[16,128,256]{1,2,0:T(8,128)(2,1)S(1)} %all-to-all-done.7) | copy-start | bytes 3145732
  342.1 67.4 %all-to-all-start.8 = ((f32[16,2,128,2,128]{4,2,3,1,0:T(8,128)}), f32[16,2,128,2,128]{4,2,3,1,0:T(8,128)}, u32[]{:S(2)}, u32[]{:S(2)}) async-start(f32[16,2,128,2,128]{4,2,3,1,0:T(8,128)} %multiply_bitcast_fusion.1), calls=%async_computation.8 | async-start | bytes 8388608 | tf_op jit(solution)/shard_map/all_to_all | solution.py:138
  353.6 61.3 %copy-start.1 = (bf16[128,16,256]{0,2,1:T(8,128)(2,1)S(1)}, bf16[128,16,256]{0,2,1:T(8,128)(2,1)}, u32[]{:S(2)}) copy-start(bf16[128,16,256]{0,2,1:T(8,128)(2,1)} %copy-done) | copy-start | bytes 3145732
  409.5 67.1 %all-to-all-start.10 = ((f32[16,2,128,2,128]{2,4,3,1,0:T(8,128)}), f32[16,2,128,2,128]{2,4,3,1,0:T(8,128)}, u32[]{:S(2)}, u32[]{:S(2)}) async-start(f32[16,2,128,2,128]{2,4,3,1,0:T(8,128)} %convolution_bitcast_fusion.1), calls=%async_computation.10 | async-start | bytes 8388608 | tf_op jit(solution)/shard_map/all_to_all | solution.py:139
  437.5 43.7 %copy-start.2 = (bf16[16,128,256]{1,2,0:T(8,128)(2,1)S(1)}, bf16[16,128,256]{1,2,0:T(8,128)(2,1)}, u32[]{:S(2)}) copy-start(bf16[16,128,256]{1,2,0:T(8,128)(2,1)} %copy.376) | copy-start | bytes 3145732
  476.6 39.6 %all-to-all-start.9 = ((bf16[16,128,256]{1,2,0:T(8,128)(2,1)}), bf16[16,128,256]{1,2,0:T(8,128)(2,1)}, u32[]{:S(2)}, u32[]{:S(2)}) async-start(bf16[16,128,256]{1,2,0:T(8,128)(2,1)} %bitcast.81), calls=%async_computation.9 | async-start | bytes 2097152 | tf_op jit(solution)/shard_map/all_to_all | solution.py:147
  514.8 13.3 %copy-start.10 = (bf16[16,128,256]{1,2,0:T(8,128)(2,1)S(1)}, bf16[16,128,256]{1,2,0:T(8,128)(2,1)}, u32[]{:S(2)}) copy-start(bf16[16,128,256]{1,2,0:T(8,128)(2,1)} %copy-done.9) | copy-start | bytes 3145732
  516.2 40.3 %all-to-all-start.11 = ((bf16[16,128,256]{1,2,0:T(8,128)(2,1)}), bf16[16,128,256]{1,2,0:T(8,128)(2,1)S(1)}, u32[]{:S(2)}, u32[]{:S(2)}) async-start(bf16[16,128,256]{1,2,0:T(8,128)(2,1)} %bitcast.92), calls=%async_computation.11 | async-start | bytes 2097152 | tf_op jit(solution)/shard_map/all_to_all | solution.py:148
  (2 other events, 4.9 us)
